TPU v7x, 1024 devices: a whole 8x8x8 slice. The times are simulated.
1024 devices in a mesh: energy: 32 (over y_lo, x, core), space: 32 (over z, y_hi).
Axes of the slice: x: 8, y: 8 (y_hi: 4, y_lo: 2; y = y_hi * 2 + y_lo), z: 8, core: 2. Of those that a mesh axis runs over, the one named last changes fastest.
Arguments:
- green: bfloat16 [4, 32, 32, 384, 384], P(None, 'energy', 'space'), may hold values from -6 to 6
- v_diag: bfloat16 [32, 384, 384], P('space'), may hold values from -0.3125 to 0.3125
- v_low: bfloat16 [32, 384, 384], P('space'), may hold values from -0.3125 to 0.3125
- energy_slot: int32 [32], replicated, may hold values from 0 to 31, each once
Outputs:
- sigma: bfloat16 [2, 32, 32, 384, 384], P(None, None, 'space', 'energy')
Inputs may be any that keep to these rules, and one draw needn't show every extreme that they name: `energy_slot`: each grid energy appears in exactly one slot.
All inputs are finite; a program needn't handle non-finite values.
Results may differ from a plain program's by a relative error of at most 0.0066.
Values may be sent and summed in bfloat16 or wider, within the bound.
A program may use at most 32 MiB of HBM per device.

v0:
```python
import math

import jax
import jax.numpy as jnp
from jax import lax
from jax.sharding import PartitionSpec as P


def shifted(value, axis, steps):
    count = lax.axis_size(axis)
    leading, last = (max(0, -steps), min(count, count - steps))
    return lax.ppermute(value, axis, [(source, source + steps) for source in range(leading, last)])


def apply_table(table, values):
    return jnp.dot(
        table, values, precision=lax.Precision.HIGHEST, preferred_element_type=jnp.float32
    )


def spectra(cos_table, sin_table, real_part, imag_part):
    out_real = apply_table(cos_table, real_part) + apply_table(sin_table, imag_part)
    out_imag = apply_table(cos_table, imag_part) - apply_table(sin_table, real_part)
    return (out_real, out_imag)


def to_slots(cos_table, sin_table, real_part, imag_part):
    factor = 1.0 / cos_table.shape[0]
    cos_back = cos_table.T
    sin_back = sin_table.T
    out_real = (apply_table(cos_back, real_part) - apply_table(sin_back, imag_part)) * factor
    out_imag = (apply_table(cos_back, imag_part) + apply_table(sin_back, real_part)) * factor
    return (out_real, out_imag)


def sandwich(matrix, polar):
    left = jnp.einsum("ij,cejk->ceik", matrix, polar, preferred_element_type=jnp.float32).astype(
        jnp.bfloat16
    )
    return jnp.einsum("ceij,kj->ceik", left, matrix, preferred_element_type=jnp.float32)


def sandwich_t(matrix, polar):
    left = jnp.einsum("ji,cejk->ceik", matrix, polar, preferred_element_type=jnp.float32).astype(
        jnp.bfloat16
    )
    return jnp.einsum("ceij,jk->ceik", left, matrix, preferred_element_type=jnp.float32)


def shards(green, v_diag, v_low, energy_slot):
    energies = energy_slot.shape[0]
    period = 2 * energies
    frequency = jnp.arange(period, dtype=jnp.int32)
    phases = frequency[:, None] * energy_slot[None, :] % period
    angles = phases.astype(jnp.float32) * (2.0 * math.pi / period)
    cos_table = jnp.cos(angles)
    sin_table = jnp.sin(angles)
    scaling = energies ** (-0.5)
    arrived = lax.all_to_all(green[:, :, 0], "energy", split_axis=2, concat_axis=1, tiled=True)
    row_count = arrived.shape[2]
    col_count = arrived.shape[3]
    flattened = arrived.reshape((4, energies, row_count * col_count)).astype(jnp.float32)
    lesser_re, lesser_im = spectra(cos_table, sin_table, flattened[0], flattened[1])
    greater_re, greater_im = spectra(cos_table, sin_table, flattened[2], flattened[3])
    cross_re = lesser_re * greater_re + lesser_im * greater_im
    cross_im = lesser_im * greater_re - lesser_re * greater_im
    corr_re, corr_im = to_slots(cos_table, sin_table, cross_re, cross_im)
    polar_slot = (
        jnp.stack([corr_im * scaling, -corr_re * scaling])
        .reshape((2, energies, row_count, col_count))
        .astype(jnp.bfloat16)
    )
    polar = lax.all_to_all(polar_slot, "energy", split_axis=1, concat_axis=2, tiled=True)
    diagonal = v_diag[0]
    lower = v_low[0]
    own_term = sandwich(diagonal, polar)
    below = shifted(polar, "space", 1)
    packed = jnp.concatenate([polar.reshape((-1,) + polar.shape[2:]), lower[None]], axis=0)
    upper = shifted(packed, "space", -1)
    above = upper[:-1].reshape(polar.shape)
    coupling_up = upper[-1]
    upper_term = lax.optimization_barrier(
        sandwich_t(coupling_up, above).astype(jnp.bfloat16)
    ).astype(jnp.float32)
    total = own_term + sandwich(lower, below) + upper_term
    screened = total.astype(jnp.bfloat16)
    screened_rows = lax.all_to_all(screened, "energy", split_axis=2, concat_axis=1, tiled=True)
    weights = screened_rows.reshape((2, energies, row_count * col_count)).astype(jnp.float32)
    weight_re, weight_im = spectra(cos_table, sin_table, weights[0], weights[1])
    joint_re = lesser_re * weight_re - lesser_im * weight_im
    joint_im = lesser_re * weight_im + lesser_im * weight_re
    conv_re, conv_im = to_slots(cos_table, sin_table, joint_re, joint_im)
    sigma = (
        jnp.stack([-conv_im * scaling, conv_re * scaling])
        .reshape((2, energies, row_count, col_count))
        .astype(jnp.bfloat16)
    )
    return sigma[:, :, None]


def solution(mesh):
    in_specs = (
        P(None, "energy", "space", None, None),
        P("space", None, None),
        P("space", None, None),
        P(),
    )
    out_specs = P(None, None, "space", "energy", None)
    return jax.shard_map(shards, mesh=mesh, in_specs=in_specs, out_specs=out_specs, check_vma=False)
```

profile of v0, /device:TPU:1, one launch (start us, length us, event | category | flops | bytes accessed | tf_op | source)
XLA Modules:
  0.0 185.6 jit_solution(9591160373722871747)
XLA Ops:
  0.0 2.2 %copy.55 = bf16[4,1,1,384,384]{4,0,3,2,1:T(4,128)(2,1)S(1)} copy(bf16[4,1,1,384,384]{4,3,2,1,0:T(8,128)(2,1)} %param.4) | data formatting | bytes 2359296 | tf_op args[0]
  2.2 48.5 %all_to_all.30 = bf16[4,1,384,384]{3,0,1,2:T(4,128)(2,1)S(1)} all-to-all(bf16[4,1,384,384]{3,0,1,2:T(4,128)(2,1)S(1)} %bitcast.82), channel_id=1, replica_groups=mesh['energy'=32,'space'=32] {'energy'}, dimensions={2} | all-to-all | bytes 2359296 | tf_op jit(solution)/shard_map/all_to_all | solution.py:59
  50.7 8.2 %slice_reduce_fusion.3 = (bf16[384,384]{1,0:T(8,128)(2,1)S(1)}, bf16[384,384]{1,0:T(8,128)(2,1)}, bf16[384,384]{1,0:T(8,128)(2,1)S(1)}, bf16[384,384]{1,0:T(8,128)(2,1)S(1)}) fusion(bf16[4,1,384,384]{3,0,1,2:T(4,128)(2,1)S(1)} %all_to_all.30), kind=kLoop, calls=%fused_computation.46 | loop fusion | bytes 2359296 | tf_op jit(solution)/shard_map/slice | solution.py:64
  60.4 1.7 fusion.52
  64.0 1.3 squeeze.34
  68.1 2.2 %multiply_subtract_fusion.1 = (f32[64,4608]{1,0:T(8,128)S(1)}, f32[64,4608]{1,0:T(8,128)S(1)}, f32[64,4608]{1,0:T(8,128)}) fusion(f32[64,4608]{1,0:T(8,128)S(1)} %convolution_subtract_fusion.1, f32[64,4608]{1,0:T(8,128)S(1)} %convolution_subtract_fusion.2, f32[64,4608]{1,0:T(8,128)S(1)} %convolution_add_fusion.1, f32[64,4608]{1,0:T(8,128)S(1)} %copy-done.1, ...), kind=kOutput, calls=%fused_computation.39 | convolution fusion | flops 115339264 | bytes 8552576 | tf_op jit(solution)/shard_map/dot_general | solution.py:16
  72.8 1.0 stack.18
  73.7 1.6 fusion.9
  75.3 1.2 stack.19
  76.5 1.2 pad_maximum_fusion.1
  78.3 22.2 %all_to_all.31 = bf16[2,32,12,384]{3,0,2,1:T(2,128)(2,1)S(1)} all-to-all(bf16[2,32,12,384]{3,0,2,1:T(2,128)(2,1)S(1)} %copy.37), channel_id=1, replica_groups=mesh['energy'=32,'space'=32] {'energy'}, dimensions={1} | all-to-all | bytes 1179648 | tf_op jit(solution)/shard_map/all_to_all | solution.py:73
  100.6 1.0 pad_maximum_fusion
  101.6 1.3 collective-permute-start.1
  102.9 1.0 copy.40
  103.9 5.7 %collective-permute-start = (bf16[2,1,384,384]{2,3,0,1:T(8,128)(2,1)S(1)}, bf16[2,1,384,384]{2,3,0,1:T(8,128)(2,1)}, u32[]{:S(2)}, u32[]{:S(2)}) collective-permute-start(bf16[2,1,384,384]{2,3,0,1:T(8,128)(2,1)S(1)} %copy.40), channel_id=1, source_target_pairs={{0,1},{1,2},{2,3},{3,4},{4,5},{5,6},{6,7},{7,8},{8,9},{9,10},{10,1... | collective-permute-start | bytes 1769480 | tf_op jit(solution)/shard_map/ppermute | solution.py:12
  109.6 2.1 %fusion.18 = f32[2,384,384]{2,1,0:T(8,128)} fusion(bf16[1,384,384]{2,1,0:T(8,128)(2,1)S(1)} %copy-done, bf16[2,384,384]{2,0,1:T(2,128)(2,1)S(1)} %bitcast.81), kind=kOutput, calls=%fused_computation.33 | convolution fusion | flops 453279744 | bytes 2064384 | tf_op jit(solution)/shard_map/ceij,kj->ceik/dot_general | solution.py:40
  111.7 29.5 %collective-permute-done.1 = bf16[3,384,384]{2,1,0:T(8,128)(2,1)} collective-permute-done((bf16[3,384,384]{2,1,0:T(8,128)(2,1)}, bf16[3,384,384]{2,1,0:T(8,128)(2,1)}, u32[]{:S(2)}, u32[]{:S(2)}) %collective-permute-start.1) | collective-permute-done | bytes 884768 | tf_op jit(solution)/shard_map/ppermute | solution.py:12
  141.2 3.1 %fusion.16 = bf16[2,1,384,384]{3,2,0,1:T(8,128)(2,1)} fusion(bf16[3,384,384]{2,1,0:T(8,128)(2,1)} %collective-permute-done.1), kind=kOutput, calls=%fused_computation.31 | convolution fusion | flops 453574656 | bytes 2064384 | tf_op jit(solution)/shard_map/ceij,jk->ceik/dot_general | solution.py:47
  144.3 2.3 %fusion.14 = bf16[2,1,384,384]{3,2,0,1:T(8,128)(2,1)S(1)} fusion(f32[2,384,384]{2,1,0:T(8,128)S(1)} %copy-done.2, bf16[2,1,384,384]{3,2,0,1:T(8,128)(2,1)} %fusion.16, bf16[2,1,384,384]{2,3,0,1:T(8,128)(2,1)} %collective-permute-done, bf16[1,384,384]{2,1,0:T(8,128)(2,1)S(1)} %copy-done.4), kind=kOutput, calls=%fused_computation.28 | convolution fusion | flops 454459392 | bytes 3244032 | tf_op jit(solution)/shard_map/ceij,kj->ceik/dot_general | solution.py:40
  147.3 25.9 %all_to_all.32 = bf16[2,1,384,384]{3,0,1,2:T(2,128)(2,1)S(1)} all-to-all(bf16[2,1,384,384]{3,0,1,2:T(2,128)(2,1)S(1)} %copy.45), channel_id=1, replica_groups=mesh['energy'=32,'space'=32] {'energy'}, dimensions={2} | all-to-all | bytes 1179648 | tf_op jit(solution)/shard_map/all_to_all | solution.py:87
  173.2 2.9 %slice_reduce_fusion = (bf16[384,384]{1,0:T(8,128)(2,1)S(1)}, bf16[384,384]{1,0:T(8,128)(2,1)S(1)}) fusion(bf16[2,1,384,384]{3,0,1,2:T(2,128)(2,1)S(1)} %all_to_all.32), kind=kLoop, calls=%fused_computation.43 | loop fusion | bytes 1179648 | tf_op jit(solution)/shard_map/slice | solution.py:89
  179.6 1.1 multiply_add_fusion
  182.4 0.8 fusion.8
  184.7 0.9 copy.46
  (39 shorter events, 16.3 us)
Async XLA Ops:
  0.0 109.6 %copy-start = (bf16[1,384,384]{2,1,0:T(8,128)(2,1)S(1)}, bf16[1,384,384]{2,1,0:T(8,128)(2,1)}, u32[]{:S(2)}) copy-start(bf16[1,384,384]{2,1,0:T(8,128)(2,1)} %param.5) | copy-start | bytes 884740
  58.9 0.7 copy-start.5
  66.8 1.3 copy-start.1
  78.2 22.3 %copy-start.4 = (bf16[1,384,384]{2,1,0:T(8,128)(2,1)S(1)}, bf16[1,384,384]{2,1,0:T(8,128)(2,1)}, u32[]{:S(2)}) copy-start(bf16[1,384,384]{2,1,0:T(8,128)(2,1)} %param.6) | copy-start | bytes 884740
  101.6 39.6 %collective-permute-start.1 = (bf16[3,384,384]{2,1,0:T(8,128)(2,1)}, bf16[3,384,384]{2,1,0:T(8,128)(2,1)}, u32[]{:S(2)}, u32[]{:S(2)}) collective-permute-start(bf16[3,384,384]{2,1,0:T(8,128)(2,1)} %pad_maximum_fusion), channel_id=1, source_target_pairs={{1,0},{2,1},{3,2},{4,3},{5,4},{6,5},{7,6},{8,7},{9,8},{10,9},{11,1... | collective-permute-start | bytes 2654216 | tf_op jit(solution)/shard_map/ppermute | solution.py:12
  103.9 40.5 %collective-permute-start = (bf16[2,1,384,384]{2,3,0,1:T(8,128)(2,1)S(1)}, bf16[2,1,384,384]{2,3,0,1:T(8,128)(2,1)}, u32[]{:S(2)}, u32[]{:S(2)}) collective-permute-start(bf16[2,1,384,384]{2,3,0,1:T(8,128)(2,1)S(1)} %copy.40), channel_id=1, source_target_pairs={{0,1},{1,2},{2,3},{3,4},{4,5},{5,6},{6,7},{7,8},{8,9},{9,10},{10,1... | collective-permute-start | bytes 1769480 | tf_op jit(solution)/shard_map/ppermute | solution.py:12
  111.7 32.6 %copy-start.2 = (f32[2,384,384]{2,1,0:T(8,128)S(1)}, f32[2,384,384]{2,1,0:T(8,128)}, u32[]{:S(2)}) copy-start(f32[2,384,384]{2,1,0:T(8,128)} %fusion.18) | copy-start | bytes 3538948
  178.3 1.3 copy-start.3
where the time goes:
time: 187 us; the launch traced here: 186 us
  blocking collectives  96.6 us (52%)
  waiting for transfers between devices  29.5 us (16%)
  matrix products  26.6 us (14%)
  local copies, waits for them, and re-layouts  23.3 us (12%)
  starting transfers between devices  6.99 us (4%)
  other arithmetic  2.34 us (1%)
    all_to_all x1, blocking collectives, shards(): lax.all_to_all(green[:, :, 0], 'energy', split_axis=2, concat_axis=1, til...  48.5 us
    ppermute x2, waiting for transfers between devices, shifted(): lax.ppermute(value, axis, [(source, source + steps) for source in range(l...  29.5 us
    all_to_all x1, blocking collectives, shards(): lax.all_to_all(screened, 'energy', split_axis=2, concat_axis=1, tiled=True)  25.9 us
    all_to_all x1, blocking collectives, shards(): lax.all_to_all(polar_slot, 'energy', split_axis=1, concat_axis=2, tiled=T...  22.2 us
    dot_general x20, matrix products, apply_table(): jnp.dot(table, values, precision=lax.Precision.HIGHEST, preferred_element...  19.1 us
    slice x1, local copies, waits for them, and re-layouts, shards(): flattened[2]  8.18 us
    ppermute x2, starting transfers between devices, shifted(): lax.ppermute(value, axis, [(source, source + steps) for source in range(l...  6.99 us
    dot_general x2, matrix products, sandwich(): jnp.einsum('ceij,kj->ceik', left, matrix, preferred_element_type=jnp.floa...  4.39 us
  transfers between devices with their start and end apart: 2, of which 1 were waited for; matrix products, arithmetic and copies ran while one was open for 3% of the time, Pallas kernels for 0%

commit v1 on v0

v1 whole, which is shorter than its diff:
```python
import functools

import jax
import jax.numpy as jnp
from jax import lax
from jax.experimental import pallas as pl
from jax.experimental.pallas import tpu as pltpu
from jax.sharding import PartitionSpec as P

F32 = jnp.float32
BF16 = jnp.bfloat16
MESH = pl.DeviceIdType.MESH
BLK = 8


def pack_green(green, chunks):
    _, size, _ = green.shape
    owners, width = size // 12, size // chunks
    g = green.reshape(2, 2, owners, 12, chunks, width).transpose(4, 2, 0, 1, 3, 5)
    top = g[:, :, :, :, :8].reshape(chunks, owners, 2, 16, width)
    low = g[:, :, :, :, 8:].reshape(chunks, owners, 2, 8, width)
    return jnp.concatenate([top, low], axis=3).reshape(chunks, owners, 48, width)


def group_index(position):
    owner = (position * 2731) >> 16
    inner = position - 24 * owner
    component = jnp.where(inner < 16, inner >> 3, (inner - 16) >> 2)
    row = jnp.where(inner < 16, inner & 7, 8 + (inner & 3))
    return component, 12 * owner + row


def dot(a, b, dims):
    return lax.dot_general(a, b, (dims, ((), ())), preferred_element_type=F32)


def kernel(ne, nb, chunks, slot_ref, green_ref, vd_ref, vl_ref, out_ref, *scratch):
    arr = scratch[0:chunks]
    abuf = scratch[chunks : 2 * chunks]
    warr = scratch[2 * chunks : 3 * chunks]
    (pout, wout, own, below, above, vup, fl, fg, grid_out, inv, spread, big_d, big_l, big_u,
     vl_own, vu_own, wacc, uacc, send_sem, recv_sem, space_send, space_recv) = scratch[3 * chunks :]
    size = vd_ref.shape[0]
    width = size // chunks
    me = lax.axis_index("energy")
    here = lax.axis_index("space")
    up = lax.rem(here + 1, nb)
    down = lax.rem(here + nb - 1, nb)
    scale = ne ** -0.5

    barrier = pltpu.get_barrier_semaphore()

    def greet(step, carry):
        peer = lax.rem(me + step, ne)
        pl.semaphore_signal(barrier, inc=1, device_id={"energy": peer, "space": here}, device_id_type=MESH)
        return carry

    lax.fori_loop(1, ne, greet, 0)
    for other in (up, down):
        pl.semaphore_signal(barrier, inc=1, device_id={"energy": me, "space": other}, device_id_type=MESH)
    pl.semaphore_wait(barrier, ne + 1)

    def to_space(src, dst, number, other):
        return pltpu.make_async_remote_copy(
            src_ref=src, dst_ref=dst, send_sem=space_send.at[number], recv_sem=space_recv.at[number],
            device_id={"energy": me, "space": other}, device_id_type=MESH)

    def exchange(phase, chunk, src, dst):
        number = phase * chunks + chunk

        def send(step, carry):
            peer = lax.rem(me + step, ne)
            pltpu.make_async_remote_copy(
                src_ref=src.at[peer], dst_ref=dst.at[me], send_sem=send_sem.at[number],
                recv_sem=recv_sem.at[number], device_id={"energy": peer, "space": here},
                device_id_type=MESH).start()
            return carry

        lax.fori_loop(1, ne, send, 0)
        pltpu.make_async_copy(src.at[me], dst.at[me], recv_sem.at[number]).start()

    def arrived(phase, chunk, dst):
        pltpu.make_async_copy(dst, dst, recv_sem.at[phase * chunks + chunk]).wait()

    def sent(phase, chunk, src):
        part = src.at[pl.ds(0, ne - 1)]
        pltpu.make_async_copy(part, part, send_sem.at[phase * chunks + chunk]).wait()

    for chunk in range(chunks):
        exchange(0, chunk, green_ref.at[chunk], arr[chunk])
    coupling = to_space(vl_ref, vup, 0, down)
    coupling.start()

    def invert(energy, carry):
        def look(slot, found):
            return jnp.where(slot_ref[slot] == energy, slot, found)

        inv[energy] = lax.fori_loop(0, ne, look, 0)
        return carry

    lax.fori_loop(0, ne, invert, 0)

    rows = 24 * ne
    _, row_of = group_index(lax.broadcasted_iota(jnp.int32, (rows, size), 0))
    spread[...] = jnp.where(row_of == lax.broadcasted_iota(jnp.int32, (rows, size), 1), 1.0, 0.0).astype(BF16)
    comp_a, _ = group_index(lax.broadcasted_iota(jnp.int32, (rows, rows), 0))
    comp_b, _ = group_index(lax.broadcasted_iota(jnp.int32, (rows, rows), 1))
    same = comp_a == comp_b

    def expand(matrix, dims):
        half = dot(spread[...], matrix, dims).astype(BF16)
        return jnp.where(same, dot(half, spread[...], ((1,), (1,))), 0.0).astype(BF16)

    big_d[...] = expand(vd_ref[...], ((1,), (0,)))
    vl_own[...] = jnp.where(here > 0, vl_ref[...], jnp.zeros_like(vl_ref))
    big_l[...] = expand(vl_own[...], ((1,), (0,)))

    zeros = jnp.zeros((BLK, 24, width), F32)
    for chunk in range(chunks):
        fl[chunk, 0:BLK] = zeros
        fl[chunk, BLK + ne : 2 * BLK + ne] = zeros
    top_rows = lax.broadcasted_iota(jnp.int32, (BLK, 8, width), 1) < 4

    def put_second(energy, value):
        fg[energy, 0:24] = value
        fg[energy, 24:32] = pltpu.roll(value[16:24], 4, 0)

    def products(window, energy, acc):
        a, b, m1, m2 = acc
        xr, xi, xm = window[:, 0:8], window[:, 8:16], window[:, 16:24]
        second = fg[energy]
        yr, yi, ym, ys = (second[8 * i : 8 * i + 8][None] for i in range(4))
        return xr, xi, yr, yi, a, b, m1 + xm * ym, m2 + xm * ys

    blank = tuple(jnp.zeros((BLK, 8, width), F32) for _ in range(4))

    def polar(chunk):
        arrived(0, chunk, arr[chunk])

        def place(energy, carry):
            value = arr[chunk][inv[energy]].astype(F32)
            fl[chunk, BLK + energy] = value[0:24]
            put_second(energy, value[24:48])
            return carry

        lax.fori_loop(0, ne, place, 0, unroll=4)
        for first in range(0, ne, BLK):
            def step(energy, acc):
                window = fl[chunk, pl.ds(BLK + first + energy, BLK)]
                xr, xi, yr, yi, a, b, m1, m2 = products(window, energy, acc)
                return a + (xi * yr - xr * yi), b + (xr * yr + xi * yi), m1, m2

            a, b, m1, m2 = lax.fori_loop(0, ne - first, step, blank, unroll=4)
            mixed = jnp.where(top_rows, pltpu.roll(m2, 4, 1) - m2, -(m1 + pltpu.roll(m1, 4, 1)))
            grid_out[first : first + BLK] = jnp.concatenate([a, -b, mixed], axis=1) * scale

        def to_slot(slot, carry):
            pout[chunk, slot] = grid_out[slot_ref[slot]].astype(BF16)
            return carry

        lax.fori_loop(0, ne, to_slot, 0, unroll=4)
        exchange(1, chunk, pout.at[chunk], abuf[chunk])

    for chunk in range(chunks):
        polar(chunk)

    coupling.wait()
    vu_own[...] = jnp.where(here < nb - 1, vup[...], jnp.zeros_like(vup))
    big_u[...] = expand(vu_own[...], ((1,), (1,)))

    copies = []
    for chunk in range(chunks):
        cols = slice(chunk * width, (chunk + 1) * width)
        arrived(1, chunk, abuf[chunk])
        own[chunk] = abuf[chunk][...].astype(F32).reshape(rows, width).astype(BF16)
        for number, dst, other in ((1 + chunk, below, up), (1 + chunks + chunk, above, down)):
            copy = to_space(own.at[chunk], dst.at[chunk], number, other)
            copy.start()
            copies.append(copy)
        left = dot(big_d[...], own[chunk], ((1,), (0,))).astype(BF16)
        part = dot(left, vd_ref[:, cols], ((1,), (1,)))
        wacc[...] = part if chunk == 0 else wacc[...] + part

    for chunk in range(chunks):
        cols = slice(chunk * width, (chunk + 1) * width)
        copies[2 * chunk].wait_recv()
        left = dot(big_l[...], below[chunk], ((1,), (0,))).astype(BF16)
        wacc[...] += dot(left, vl_own[:, cols], ((1,), (1,)))
        copies[2 * chunk + 1].wait_recv()
        left = dot(big_u[...], above[chunk], ((1,), (0,))).astype(BF16)
        part = dot(left, vu_own[cols, :], ((1,), (0,)))
        uacc[...] = part if chunk == 0 else uacc[...] + part

    for chunk in range(chunks):
        cols = slice(chunk * width, (chunk + 1) * width)
        total = wacc[:, cols] + uacc[:, cols].astype(BF16).astype(F32)
        wout[chunk] = total.reshape(ne, 24, width).astype(BF16)
        exchange(2, chunk, wout.at[chunk], warr[chunk])

    def sigma(chunk):
        cols = slice(chunk * width, (chunk + 1) * width)
        arrived(2, chunk, warr[chunk])

        def place(energy, carry):
            put_second(energy, warr[chunk][inv[energy]].astype(F32))
            return carry

        lax.fori_loop(0, ne, place, 0, unroll=4)
        for first in range(0, ne, BLK):
            def step(energy, acc):
                window = fl[chunk, pl.ds(BLK + first - energy, BLK)]
                xr, xi, yr, yi, a, b, m1, m2 = products(window, energy, acc)
                return a + (xr * yi + xi * yr), b + (xr * yr - xi * yi), m1, m2

            a, b, m1, m2 = lax.fori_loop(0, first + BLK, step, blank, unroll=4)
            mixed = jnp.where(top_rows, -(m2 + pltpu.roll(m2, 4, 1)), pltpu.roll(m1, 4, 1) - m1)
            grid_out[first : first + BLK] = jnp.concatenate([-a, b, mixed], axis=1) * scale

        def to_slot(slot, carry):
            value = grid_out[slot_ref[slot]]
            out_ref[0, slot, :, cols] = jnp.concatenate([value[0:8], value[16:20]], axis=0).astype(BF16)
            out_ref[1, slot, :, cols] = jnp.concatenate([value[8:16], value[20:24]], axis=0).astype(BF16)
            return carry

        lax.fori_loop(0, ne, to_slot, 0, unroll=4)

    for chunk in range(chunks):
        sigma(chunk)

    for copy in copies:
        copy.wait_send()
    for chunk in range(chunks):
        sent(0, chunk, green_ref.at[chunk])
        sent(1, chunk, pout.at[chunk])
        sent(2, chunk, wout.at[chunk])


def shards(ne, nb, chunks, green, v_diag, v_low, energy_slot):
    size = v_diag.shape[-1]
    width = size // chunks
    rows = 24 * ne
    packed = pack_green(green[:, 0, 0], chunks)
    vmem = pl.BlockSpec(memory_space=pltpu.VMEM)
    scratch = (
        [pltpu.VMEM((ne, 48, width), BF16)] * chunks
        + [pltpu.VMEM((ne, 24, width), BF16)] * chunks
        + [pltpu.VMEM((ne, 24, width), BF16)] * chunks
        + [
            pltpu.VMEM((chunks, ne, 24, width), BF16),
            pltpu.VMEM((chunks, ne, 24, width), BF16),
            pltpu.VMEM((chunks, rows, width), BF16),
            pltpu.VMEM((chunks, rows, width), BF16),
            pltpu.VMEM((chunks, rows, width), BF16),
            pltpu.VMEM((size, size), BF16),
            pltpu.VMEM((chunks, ne + 2 * BLK, 24, width), F32),
            pltpu.VMEM((ne, 32, width), F32),
            pltpu.VMEM((ne, 24, width), F32),
            pltpu.SMEM((ne,), jnp.int32),
            pltpu.VMEM((rows, size), BF16),
            pltpu.VMEM((rows, rows), BF16),
            pltpu.VMEM((rows, rows), BF16),
            pltpu.VMEM((rows, rows), BF16),
            pltpu.VMEM((size, size), BF16),
            pltpu.VMEM((size, size), BF16),
            pltpu.VMEM((rows, size), F32),
            pltpu.VMEM((rows, size), F32),
            pltpu.SemaphoreType.DMA((3 * chunks,)),
            pltpu.SemaphoreType.DMA((3 * chunks,)),
            pltpu.SemaphoreType.DMA((1 + 2 * chunks,)),
            pltpu.SemaphoreType.DMA((1 + 2 * chunks,)),
        ]
    )
    sigma = pl.pallas_call(
        functools.partial(kernel, ne, nb, chunks),
        out_shape=jax.ShapeDtypeStruct((2, ne, 12, size), BF16),
        in_specs=[pl.BlockSpec(memory_space=pltpu.SMEM), vmem, vmem, vmem],
        out_specs=vmem,
        scratch_shapes=scratch,
        compiler_params=pltpu.CompilerParams(
            collective_id=0, has_side_effects=True, vmem_limit_bytes=40 * 1024 * 1024
        ),
        cost_estimate=pl.CostEstimate(flops=2_500_000_000, bytes_accessed=4_000_000, transcendentals=0),
    )(energy_slot, packed, v_diag[0], v_low[0])
    return sigma[:, :, None]


def solution(mesh):
    in_specs = (
        P(None, "energy", "space", None, None),
        P("space", None, None),
        P("space", None, None),
        P(),
    )
    out_specs = P(None, None, "space", "energy", None)
    body = functools.partial(shards, mesh.shape["energy"], mesh.shape["space"], 3)
    return jax.shard_map(body, mesh=mesh, in_specs=in_specs, out_specs=out_specs, check_vma=False)
```

time: 187 us -> 116 us (0.62)
  Pallas kernels: 0 us -> 110 us
  blocking collectives: 96.6 us -> 0 us
  waiting for transfers between devices: 29.5 us -> 0 us
  matrix products: 26.6 us -> 0 us
  local copies, waits for them, and re-layouts: 23.3 us -> 6.03 us
  starting transfers between devices: 6.99 us -> 0 us
  other arithmetic: 2.34 us -> 0.21 us
    pallas_call x0 -> x1, Pallas kernels: none -> 110 us  [shards(): pl.pallas_call(functools.partial(kernel, ne, nb, chunks), out_shape=jax.S...]
    all_to_all x3 -> x0, blocking collectives: 96.6 us -> none  [the longest x1 48.5 us: shards(): lax.all_to_all(green[:, :, 0], 'energy', split_axis=2, concat_axis=1, til...]
    ppermute x2 -> x0, waiting for transfers between devices: 29.5 us -> none  [shifted(): lax.ppermute(value, axis, [(source, source + steps) for source in range(l...]
    dot_general x23 -> x0, matrix products: 26.6 us -> none  [the longest x20 19.1 us: apply_table(): jnp.dot(table, values, precision=lax.Precision.HIGHEST, preferred_element...]
    slice x2 -> x4, local copies, waits for them, and re-layouts: 11.1 us -> 0.83 us  [the longest x2 0.53 us: pack_green(): top = g[:, :, :, :, :8].reshape(chunks, owners, 2, 16, width)]
    ppermute x2 -> x0, starting transfers between devices: 6.99 us -> none  [shifted(): lax.ppermute(value, axis, [(source, source + steps) for source in range(l...]
    squeeze x6 -> x0, local copies, waits for them, and re-layouts: 3.12 us -> none  [the longest x1 1.32 us: shards(): flattened[3]]
    unnamed x13 -> x6, local copies, waits for them, and re-layouts: 3.24 us -> 0.82 us
  transfers between devices with their start and end apart: 2 -> 0, of which waited for: 1 -> 0; matrix products, arithmetic and copies ran while one was open for 3% -> 0% of each run, Pallas kernels for 0% -> 0%
where the time goes in v1:
time: 116 us
  Pallas kernels  110 us (95%)
  local copies, waits for them, and re-layouts  6.03 us (5%)
    pallas_call x1, Pallas kernels, shards(): pl.pallas_call(functools.partial(kernel, ne, nb, chunks), out_shape=jax.S...  110 us
    another operation x1, local copies, waits for them, and re-layouts, pack_green(): green.reshape(2, 2, owners, 12, chunks, width).transpose(4, 2, 0, 1, 3, 5)  3.29 us

profile of v1, /device:TPU:1, one launch (start us, length us, event | category | flops | bytes accessed | tf_op | source)
XLA Modules:
  0.0 115.9 jit_solution(9403559421494314032)
XLA Ops:
  0.0 3.3 %reshape_squeeze.3 = bf16[2,2,32,12,3,128]{5,4,3,2,1,0:T(4,128)(2,1)S(1)} reshape(bf16[4,1,1,384,384]{4,3,2,1,0:T(8,128)(2,1)} %param.4) | data formatting | bytes 2359296 | tf_op jit(solution)/shard_map/reshape;squeeze | solution.py:19
  3.3 0.2 slice.9
  3.5 0.1 copy.10
  3.6 0.2 copy.11
  3.8 0.4 slice.8
  4.2 0.1 copy.14
  4.3 0.0 copy-start
  4.3 0.0 copy-start.1
  4.3 0.0 copy-start.2
  4.4 0.2 pad_maximum_fusion
  4.6 0.7 copy-done
  5.3 0.1 copy-done.1
  5.4 0.0 copy-done.2
  5.4 109.6 %shard_map.46 = bf16[2,32,12,384]{3,2,1,0:T(8,128)(2,1)S(1)} custom-call(s32[32]{0:T(128)S(1)} %copy-done.2, bf16[3,32,48,128]{3,2,1,0:T(8,128)(2,1)S(1)} %bitcast.11, bf16[384,384]{1,0:T(8,128)(2,1)S(1)} %bitcast.13, bf16[384,384]{1,0:T(8,128)(2,1)S(1)} %bitcast.14), custom_call_target="tpu_custom_call" | custom-call | flops 2500000000 | bytes 4000000 | tf_op jit(solution)/shard_map/pallas_call | solution.py:273
  115.0 0.9 copy.12
Async XLA Ops:
  4.3 1.0 copy-start
  4.3 1.0 copy-start.1
  4.3 1.0 copy-start.2

commit v2 on v1

--- a/solution.py
+++ b/solution.py
@@ -13,13 +13,18 @@
 BLK = 8
 
 
-def pack_green(green, chunks):
-    _, size, _ = green.shape
-    owners, width = size // 12, size // chunks
-    g = green.reshape(2, 2, owners, 12, chunks, width).transpose(4, 2, 0, 1, 3, 5)
-    top = g[:, :, :, :, :8].reshape(chunks, owners, 2, 16, width)
-    low = g[:, :, :, :, 8:].reshape(chunks, owners, 2, 8, width)
-    return jnp.concatenate([top, low], axis=3).reshape(chunks, owners, 48, width)
+def pack_green(green_ref, packed, cols):
+    def four_owners(quad, carry):
+        rows = pl.ds(pl.multiple_of(48 * quad, 48), 48)
+        parts = [green_ref[part, rows, cols].astype(F32) for part in range(4)]
+        for i in range(4):
+            top = [part[12 * i : 12 * i + 8] for part in parts]
+            end = [part[12 * i + 8 : 12 * i + 12] for part in parts]
+            value = jnp.concatenate([top[0], top[1], end[0], end[1], top[2], top[3], end[2], end[3]], axis=0)
+            packed[4 * quad + i] = value.astype(BF16)
+        return carry
+
+    lax.fori_loop(0, green_ref.shape[1] // 48, four_owners, 0)
 
 
 def group_index(position):
@@ -38,7 +43,7 @@
     arr = scratch[0:chunks]
     abuf = scratch[chunks : 2 * chunks]
     warr = scratch[2 * chunks : 3 * chunks]
-    (pout, wout, own, below, above, vup, fl, fg, grid_out, inv, spread, big_d, big_l, big_u,
+    (packed, pout, wout, own, below, above, vup, fl, fg, grid_out, inv, spread, big_d, big_l, big_u,
      vl_own, vu_own, wacc, uacc, send_sem, recv_sem, space_send, space_recv) = scratch[3 * chunks :]
     size = vd_ref.shape[0]
     width = size // chunks
@@ -58,6 +63,11 @@
     lax.fori_loop(1, ne, greet, 0)
     for other in (up, down):
         pl.semaphore_signal(barrier, inc=1, device_id={"energy": me, "space": other}, device_id_type=MESH)
+
+    def pack(chunk):
+        pack_green(green_ref, packed.at[chunk], slice(chunk * width, (chunk + 1) * width))
+
+    pack(0)
     pl.semaphore_wait(barrier, ne + 1)
 
     def to_space(src, dst, number, other):
@@ -86,10 +96,14 @@
         part = src.at[pl.ds(0, ne - 1)]
         pltpu.make_async_copy(part, part, send_sem.at[phase * chunks + chunk]).wait()
 
-    for chunk in range(chunks):
-        exchange(0, chunk, green_ref.at[chunk], arr[chunk])
+    exchange(0, 0, packed.at[0], arr[0])
+    for chunk in range(1, min(2, chunks)):
+        pack(chunk)
+        exchange(0, chunk, packed.at[chunk], arr[chunk])
     coupling = to_space(vl_ref, vup, 0, down)
     coupling.start()
+    for chunk in range(2, chunks):
+        pack(chunk)
 
     def invert(energy, carry):
         def look(slot, found):
@@ -161,25 +175,35 @@
         lax.fori_loop(0, ne, to_slot, 0, unroll=4)
         exchange(1, chunk, pout.at[chunk], abuf[chunk])
 
-    for chunk in range(chunks):
-        polar(chunk)
-
-    coupling.wait()
-    vu_own[...] = jnp.where(here < nb - 1, vup[...], jnp.zeros_like(vup))
-    big_u[...] = expand(vu_own[...], ((1,), (1,)))
-
     copies = []
-    for chunk in range(chunks):
-        cols = slice(chunk * width, (chunk + 1) * width)
+
+    def pass_on(chunk):
         arrived(1, chunk, abuf[chunk])
         own[chunk] = abuf[chunk][...].astype(F32).reshape(rows, width).astype(BF16)
         for number, dst, other in ((1 + chunk, below, up), (1 + chunks + chunk, above, down)):
             copy = to_space(own.at[chunk], dst.at[chunk], number, other)
             copy.start()
             copies.append(copy)
+
+    def own_products(chunk):
+        cols = slice(chunk * width, (chunk + 1) * width)
         left = dot(big_d[...], own[chunk], ((1,), (0,))).astype(BF16)
         part = dot(left, vd_ref[:, cols], ((1,), (1,)))
         wacc[...] = part if chunk == 0 else wacc[...] + part
+
+    for chunk in range(chunks):
+        polar(chunk)
+        if chunk + 2 < chunks:
+            exchange(0, chunk + 2, packed.at[chunk + 2], arr[chunk + 2])
+        if chunk > 0:
+            pass_on(chunk - 1)
+
+    coupling.wait()
+    vu_own[...] = jnp.where(here < nb - 1, vup[...], jnp.zeros_like(vup))
+    big_u[...] = expand(vu_own[...], ((1,), (1,)))
+    pass_on(chunks - 1)
+    for chunk in range(chunks):
+        own_products(chunk)
 
     for chunk in range(chunks):
         cols = slice(chunk * width, (chunk + 1) * width)
@@ -230,7 +254,7 @@
     for copy in copies:
         copy.wait_send()
     for chunk in range(chunks):
-        sent(0, chunk, green_ref.at[chunk])
+        sent(0, chunk, packed.at[chunk])
         sent(1, chunk, pout.at[chunk])
         sent(2, chunk, wout.at[chunk])
 
@@ -239,13 +263,13 @@
     size = v_diag.shape[-1]
     width = size // chunks
     rows = 24 * ne
-    packed = pack_green(green[:, 0, 0], chunks)
     vmem = pl.BlockSpec(memory_space=pltpu.VMEM)
     scratch = (
         [pltpu.VMEM((ne, 48, width), BF16)] * chunks
         + [pltpu.VMEM((ne, 24, width), BF16)] * chunks
         + [pltpu.VMEM((ne, 24, width), BF16)] * chunks
         + [
+            pltpu.VMEM((chunks, ne, 48, width), BF16),
             pltpu.VMEM((chunks, ne, 24, width), BF16),
             pltpu.VMEM((chunks, ne, 24, width), BF16),
             pltpu.VMEM((chunks, rows, width), BF16),
@@ -280,7 +304,7 @@
             collective_id=0, has_side_effects=True, vmem_limit_bytes=40 * 1024 * 1024
         ),
         cost_estimate=pl.CostEstimate(flops=2_500_000_000, bytes_accessed=4_000_000, transcendentals=0),
-    )(energy_slot, packed, v_diag[0], v_low[0])
+    )(energy_slot, green[:, 0, 0], v_diag[0], v_low[0])
     return sigma[:, :, None]
 
 

time: 116 us -> 109 us (0.940)
  Pallas kernels: 110 us -> 104 us
  local copies, waits for them, and re-layouts: 6.03 us -> 4.78 us
    pallas_call x1, Pallas kernels: 110 us -> 104 us  [shards(): pl.pallas_call(functools.partial(kernel, ne, nb, chunks), out_shape=jax.S...]
    another operation x1 -> x0, local copies, waits for them, and re-layouts: 3.29 us -> none  [pack_green(): green.reshape(2, 2, owners, 12, chunks, width).transpose(4, 2, 0, 1, 3, 5)]
    unnamed x6 -> x8, local copies, waits for them, and re-layouts: 0.82 us -> 3.85 us
where the time goes in v2:
time: 109 us
  Pallas kernels  104 us (95%)
  local copies, waits for them, and re-layouts  4.78 us (4%)
    pallas_call x1, Pallas kernels, shards(): pl.pallas_call(functools.partial(kernel, ne, nb, chunks), out_shape=jax.S...  104 us
    unnamed x8, local copies, waits for them, and re-layouts  3.85 us

profile of v2, /device:TPU:1, one launch (start us, length us, event | category | flops | bytes accessed | tf_op | source)
XLA Modules:
  0.0 108.7 jit_solution(8384828971805708373)
XLA Ops:
  0.0 0.0 copy-start
  0.0 1.3 %copy-done = bf16[4,1,1,384,384]{4,3,2,1,0:T(8,128)(2,1)S(1)} copy-done((bf16[4,1,1,384,384]{4,3,2,1,0:T(8,128)(2,1)S(1)}, bf16[4,1,1,384,384]{4,3,2,1,0:T(8,128)(2,1)}, u32[]{:S(2)}) %copy-start) | copy-done | bytes 1179672
  1.3 0.0 copy-start.1
  1.3 1.0 copy-done.1
  2.2 0.0 copy-start.2
  2.2 1.0 copy-done.2
  3.2 0.0 copy-start.3
  3.2 0.7 copy-done.3
  3.9 103.9 %shard_map.46 = bf16[2,32,12,384]{3,2,1,0:T(8,128)(2,1)S(1)} custom-call(s32[32]{0:T(128)S(1)} %copy-done.3, bf16[4,384,384]{2,1,0:T(8,128)(2,1)S(1)} %bitcast.5, bf16[384,384]{1,0:T(8,128)(2,1)S(1)} %bitcast.6, bf16[384,384]{1,0:T(8,128)(2,1)S(1)} %bitcast.7), custom_call_target="tpu_custom_call" | custom-call | flops 2500000000 | bytes 4000000 | tf_op jit(solution)/shard_map/pallas_call | solution.py:297
  107.7 0.9 copy.5
Async XLA Ops:
  0.0 1.3 %copy-start = (bf16[4,1,1,384,384]{4,3,2,1,0:T(8,128)(2,1)S(1)}, bf16[4,1,1,384,384]{4,3,2,1,0:T(8,128)(2,1)}, u32[]{:S(2)}) copy-start(bf16[4,1,1,384,384]{4,3,2,1,0:T(8,128)(2,1)} %param.4) | copy-start | bytes 3538948
  1.3 1.0 copy-start.1
  2.2 1.0 copy-start.2
  3.2 0.7 copy-start.3

commit v3 on v2

--- a/solution.py
+++ b/solution.py
@@ -39,11 +39,11 @@
     return lax.dot_general(a, b, (dims, ((), ())), preferred_element_type=F32)
 
 
-def kernel(ne, nb, chunks, slot_ref, green_ref, vd_ref, vl_ref, out_ref, *scratch):
+def kernel(ne, nb, chunks, slot_ref, green_hbm, vd_hbm, vl_hbm, out_ref, *scratch):
     arr = scratch[0:chunks]
     abuf = scratch[chunks : 2 * chunks]
     warr = scratch[2 * chunks : 3 * chunks]
-    (packed, pout, wout, own, below, above, vup, fl, fg, grid_out, inv, spread, big_d, big_l, big_u,
+    (green_ref, vd_ref, vl_ref, local_sem, packed, pout, wout, own, below, above, vup, fl, fg, grid_out, inv, spread, big_d, big_l, big_u,
      vl_own, vu_own, wacc, uacc, send_sem, recv_sem, space_send, space_recv) = scratch[3 * chunks :]
     size = vd_ref.shape[0]
     width = size // chunks
@@ -53,6 +53,13 @@
     down = lax.rem(here + nb - 1, nb)
     scale = ne ** -0.5
 
+    loads = [
+        pltpu.make_async_copy(src, dst, local_sem.at[i])
+        for i, (src, dst) in enumerate(((green_hbm, green_ref), (vd_hbm, vd_ref), (vl_hbm, vl_ref)))
+    ]
+    for load in loads:
+        load.start()
+
     barrier = pltpu.get_barrier_semaphore()
 
     def greet(step, carry):
@@ -67,6 +74,7 @@
     def pack(chunk):
         pack_green(green_ref, packed.at[chunk], slice(chunk * width, (chunk + 1) * width))
 
+    loads[0].wait()
     pack(0)
     pl.semaphore_wait(barrier, ne + 1)
 
@@ -100,8 +108,14 @@
     for chunk in range(1, min(2, chunks)):
         pack(chunk)
         exchange(0, chunk, packed.at[chunk], arr[chunk])
-    coupling = to_space(vl_ref, vup, 0, down)
+    core = lax.rem(me, 2)
+    half = pl.ds(pl.multiple_of(core * (size // 2), size // 2), size // 2)
+    coupling = to_space(vl_hbm.at[half], vup.at[half], 0, down)
     coupling.start()
+    swap = pltpu.make_async_remote_copy(
+        src_ref=vup.at[half], dst_ref=vup.at[half], send_sem=space_send.at[1 + 2 * chunks],
+        recv_sem=space_recv.at[1 + 2 * chunks], device_id={"energy": me + 1 - 2 * core, "space": here},
+        device_id_type=MESH)
     for chunk in range(2, chunks):
         pack(chunk)
 
@@ -115,8 +129,6 @@
     lax.fori_loop(0, ne, invert, 0)
 
     rows = 24 * ne
-    _, row_of = group_index(lax.broadcasted_iota(jnp.int32, (rows, size), 0))
-    spread[...] = jnp.where(row_of == lax.broadcasted_iota(jnp.int32, (rows, size), 1), 1.0, 0.0).astype(BF16)
     comp_a, _ = group_index(lax.broadcasted_iota(jnp.int32, (rows, rows), 0))
     comp_b, _ = group_index(lax.broadcasted_iota(jnp.int32, (rows, rows), 1))
     same = comp_a == comp_b
@@ -125,9 +137,15 @@
         half = dot(spread[...], matrix, dims).astype(BF16)
         return jnp.where(same, dot(half, spread[...], ((1,), (1,))), 0.0).astype(BF16)
 
-    big_d[...] = expand(vd_ref[...], ((1,), (0,)))
-    vl_own[...] = jnp.where(here > 0, vl_ref[...], jnp.zeros_like(vl_ref))
-    big_l[...] = expand(vl_own[...], ((1,), (0,)))
+    def prepare():
+        _, row_of = group_index(lax.broadcasted_iota(jnp.int32, (rows, size), 0))
+        spread[...] = jnp.where(row_of == lax.broadcasted_iota(jnp.int32, (rows, size), 1), 1.0, 0.0).astype(BF16)
+        loads[1].wait()
+        loads[2].wait()
+        big_d[...] = expand(vd_ref[...], ((1,), (0,)))
+        vl_own[...] = jnp.where(here > 0, vl_ref[...], jnp.zeros_like(vl_ref))
+        big_l[...] = expand(vl_own[...], ((1,), (0,)))
+
 
     zeros = jnp.zeros((BLK, 24, width), F32)
     for chunk in range(chunks):
@@ -195,10 +213,15 @@
         polar(chunk)
         if chunk + 2 < chunks:
             exchange(0, chunk + 2, packed.at[chunk + 2], arr[chunk + 2])
+        if chunk == 0:
+            prepare()
         if chunk > 0:
             pass_on(chunk - 1)
-
-    coupling.wait()
+        if chunk == 1:
+            coupling.wait()
+            swap.start()
+
+    swap.wait()
     vu_own[...] = jnp.where(here < nb - 1, vup[...], jnp.zeros_like(vup))
     big_u[...] = expand(vu_own[...], ((1,), (1,)))
     pass_on(chunks - 1)
@@ -264,11 +287,16 @@
     width = size // chunks
     rows = 24 * ne
     vmem = pl.BlockSpec(memory_space=pltpu.VMEM)
+    hbm = pl.BlockSpec(memory_space=pltpu.HBM)
     scratch = (
         [pltpu.VMEM((ne, 48, width), BF16)] * chunks
         + [pltpu.VMEM((ne, 24, width), BF16)] * chunks
         + [pltpu.VMEM((ne, 24, width), BF16)] * chunks
         + [
+            pltpu.VMEM((4, size, size), BF16),
+            pltpu.VMEM((size, size), BF16),
+            pltpu.VMEM((size, size), BF16),
+            pltpu.SemaphoreType.DMA((3,)),
             pltpu.VMEM((chunks, ne, 48, width), BF16),
             pltpu.VMEM((chunks, ne, 24, width), BF16),
             pltpu.VMEM((chunks, ne, 24, width), BF16),
@@ -290,18 +318,18 @@
             pltpu.VMEM((rows, size), F32),
             pltpu.SemaphoreType.DMA((3 * chunks,)),
             pltpu.SemaphoreType.DMA((3 * chunks,)),
-            pltpu.SemaphoreType.DMA((1 + 2 * chunks,)),
-            pltpu.SemaphoreType.DMA((1 + 2 * chunks,)),
+            pltpu.SemaphoreType.DMA((2 + 2 * chunks,)),
+            pltpu.SemaphoreType.DMA((2 + 2 * chunks,)),
         ]
     )
     sigma = pl.pallas_call(
         functools.partial(kernel, ne, nb, chunks),
         out_shape=jax.ShapeDtypeStruct((2, ne, 12, size), BF16),
-        in_specs=[pl.BlockSpec(memory_space=pltpu.SMEM), vmem, vmem, vmem],
+        in_specs=[pl.BlockSpec(memory_space=pltpu.SMEM), hbm, hbm, hbm],
         out_specs=vmem,
         scratch_shapes=scratch,
         compiler_params=pltpu.CompilerParams(
-            collective_id=0, has_side_effects=True, vmem_limit_bytes=40 * 1024 * 1024
+            collective_id=0, has_side_effects=True, vmem_limit_bytes=56 * 1024 * 1024
         ),
         cost_estimate=pl.CostEstimate(flops=2_500_000_000, bytes_accessed=4_000_000, transcendentals=0),
     )(energy_slot, green[:, 0, 0], v_diag[0], v_low[0])

time: 109 us -> 108 us (level)
  local copies, waits for them, and re-layouts: 4.78 us -> 2.07 us
  Pallas kernels: 104 us -> 106 us
    unnamed x8 -> x0, local copies, waits for them, and re-layouts: 3.85 us -> none
    pallas_call x1, Pallas kernels: 104 us -> 106 us  [shards(): pl.pallas_call(functools.partial(kernel, ne, nb, chunks), out_shape=jax.S...]
    broadcast_in_dim x1, local copies, waits for them, and re-layouts: 0.93 us -> 2.07 us  [shards(): return sigma[:, :, None]]
where the time goes in v3:
time: 108 us
  Pallas kernels  106 us (98%)
  local copies, waits for them, and re-layouts  2.07 us (2%)
    pallas_call x1, Pallas kernels, shards(): pl.pallas_call(functools.partial(kernel, ne, nb, chunks), out_shape=jax.S...  106 us

profile of v3, /device:TPU:1, one launch (start us, length us, event | category | flops | bytes accessed | tf_op | source)
XLA Modules:
  0.0 107.9 jit_solution(5995737051287310063)
XLA Ops:
  0.0 105.8 %shard_map.46 = bf16[2,32,12,384]{3,2,1,0:T(8,128)(2,1)} custom-call(s32[32]{0:T(128)} %slot_ref.1, bf16[4,384,384]{2,1,0:T(8,128)(2,1)} %bitcast.5, bf16[384,384]{1,0:T(8,128)(2,1)} %bitcast.6, bf16[384,384]{1,0:T(8,128)(2,1)} %bitcast.7), custom_call_target="tpu_custom_call" | custom-call | flops 2500000000 | bytes 4000000 | tf_op jit(solution)/shard_map/pallas_call | solution.py:325
  105.8 2.1 %copy.5 = bf16[2,32,1,12,384]{4,1,3,2,0:T(8,128)(2,1)} copy(bf16[2,32,1,12,384]{4,3,1,0,2:T(8,128)(2,1)} %bitcast.4) | data formatting | bytes 1179648 | tf_op jit(solution)/shard_map/broadcast_in_dim | solution.py:336

commit v4 on v3

--- a/solution.py
+++ b/solution.py
@@ -175,14 +175,14 @@
             put_second(energy, value[24:48])
             return carry
 
-        lax.fori_loop(0, ne, place, 0, unroll=4)
+        lax.fori_loop(0, ne, place, 0, unroll=8)
         for first in range(0, ne, BLK):
             def step(energy, acc):
                 window = fl[chunk, pl.ds(BLK + first + energy, BLK)]
                 xr, xi, yr, yi, a, b, m1, m2 = products(window, energy, acc)
                 return a + (xi * yr - xr * yi), b + (xr * yr + xi * yi), m1, m2
 
-            a, b, m1, m2 = lax.fori_loop(0, ne - first, step, blank, unroll=4)
+            a, b, m1, m2 = lax.fori_loop(0, ne - first, step, blank, unroll=8)
             mixed = jnp.where(top_rows, pltpu.roll(m2, 4, 1) - m2, -(m1 + pltpu.roll(m1, 4, 1)))
             grid_out[first : first + BLK] = jnp.concatenate([a, -b, mixed], axis=1) * scale
 
@@ -190,7 +190,7 @@
             pout[chunk, slot] = grid_out[slot_ref[slot]].astype(BF16)
             return carry
 
-        lax.fori_loop(0, ne, to_slot, 0, unroll=4)
+        lax.fori_loop(0, ne, to_slot, 0, unroll=8)
         exchange(1, chunk, pout.at[chunk], abuf[chunk])
 
     copies = []
@@ -252,14 +252,14 @@
             put_second(energy, warr[chunk][inv[energy]].astype(F32))
             return carry
 
-        lax.fori_loop(0, ne, place, 0, unroll=4)
+        lax.fori_loop(0, ne, place, 0, unroll=8)
         for first in range(0, ne, BLK):
             def step(energy, acc):
                 window = fl[chunk, pl.ds(BLK + first - energy, BLK)]
                 xr, xi, yr, yi, a, b, m1, m2 = products(window, energy, acc)
                 return a + (xr * yi + xi * yr), b + (xr * yr - xi * yi), m1, m2
 
-            a, b, m1, m2 = lax.fori_loop(0, first + BLK, step, blank, unroll=4)
+            a, b, m1, m2 = lax.fori_loop(0, first + BLK, step, blank, unroll=8)
             mixed = jnp.where(top_rows, -(m2 + pltpu.roll(m2, 4, 1)), pltpu.roll(m1, 4, 1) - m1)
             grid_out[first : first + BLK] = jnp.concatenate([-a, b, mixed], axis=1) * scale
 
@@ -269,7 +269,7 @@
             out_ref[1, slot, :, cols] = jnp.concatenate([value[8:16], value[20:24]], axis=0).astype(BF16)
             return carry
 
-        lax.fori_loop(0, ne, to_slot, 0, unroll=4)
+        lax.fori_loop(0, ne, to_slot, 0, unroll=8)
 
     for chunk in range(chunks):
         sigma(chunk)

time: 108 us -> 107 us (level)
    pallas_call x1, Pallas kernels: 106 us -> 105 us  [shards(): pl.pallas_call(functools.partial(kernel, ne, nb, chunks), out_shape=jax.S...]
where the time goes in v4:
time: 107 us
  Pallas kernels  105 us (98%)
  local copies, waits for them, and re-layouts  2.07 us (2%)
    pallas_call x1, Pallas kernels, shards(): pl.pallas_call(functools.partial(kernel, ne, nb, chunks), out_shape=jax.S...  105 us

profile of v4, /device:TPU:1, one launch (start us, length us, event | category | flops | bytes accessed | tf_op | source)
XLA Modules:
  0.0 106.7 jit_solution(7140958795376579555)
XLA Ops:
  0.0 104.6 %shard_map.46 = bf16[2,32,12,384]{3,2,1,0:T(8,128)(2,1)} custom-call(s32[32]{0:T(128)} %slot_ref.1, bf16[4,384,384]{2,1,0:T(8,128)(2,1)} %bitcast.5, bf16[384,384]{1,0:T(8,128)(2,1)} %bitcast.6, bf16[384,384]{1,0:T(8,128)(2,1)} %bitcast.7), custom_call_target="tpu_custom_call" | custom-call | flops 2500000000 | bytes 4000000 | tf_op jit(solution)/shard_map/pallas_call | solution.py:325
  104.6 2.1 %copy.5 = bf16[2,32,1,12,384]{4,1,3,2,0:T(8,128)(2,1)} copy(bf16[2,32,1,12,384]{4,3,1,0,2:T(8,128)(2,1)} %bitcast.4) | data formatting | bytes 1179648 | tf_op jit(solution)/shard_map/broadcast_in_dim | solution.py:336
